TPU v7x, 32 devices: a whole 2x2x4 slice. The times are simulated.
32 devices in a mesh: batch: 8 (over y, x, core), blk: 4 (over z).
Axes of the slice: x: 2, y: 2, z: 4, core: 2. Of those that a mesh axis runs over, the one named last changes fastest.
Arguments:
- tokens: bfloat16 [16, 1024, 512], P('batch', 'blk'), may hold values from -6 to 6
- lengths: int32 [16], P('batch'), may hold values from 256 to 1024, as said below
- w_query: bfloat16 [512, 512], replicated, may hold values from -0.25 to 0.25
- w_key: bfloat16 [512, 512], replicated, may hold values from -0.25 to 0.25
- w_value: bfloat16 [512, 512], replicated, may hold values from -0.25 to 0.25
- w_out: bfloat16 [512, 512], replicated, may hold values from -1 to 1
- w_in: bfloat16 [512, 2048], replicated, may hold values from -0.25 to 0.25
- b_in: float32 [2048], replicated, may hold values from -3 to 3
- w_back: bfloat16 [2048, 512], replicated, may hold values from -0.125 to 0.125
- b_back: float32 [512], replicated, may hold values from -3 to 3
- alpha_attn: float32 [], replicated, may hold values from 0.3 to 1.2
- alpha_ffn: float32 [], replicated, may hold values from 0.3 to 1.2
- cotangent: bfloat16 [16, 1024, 512], P('batch', 'blk'), may hold values from -6 to 6
Outputs:
- outputs: bfloat16 [16, 1024, 512], P('batch', 'blk')
- grad_input: bfloat16 [16, 1024, 512], P('batch', 'blk')
- grad_w_query: float32 [512, 512], replicated
- grad_w_key: float32 [512, 512], replicated
- grad_w_value: float32 [512, 512], replicated
- grad_w_out: float32 [512, 512], replicated
- grad_w_in: float32 [512, 2048], replicated
- grad_b_in: float32 [2048], replicated
- grad_w_back: float32 [2048, 512], replicated
- grad_b_back: float32 [512], replicated
- grad_alpha_attn: float32 [], replicated
- grad_alpha_ffn: float32 [], replicated
Inputs may be any that keep to these rules, and one draw needn't show every extreme that they name: `lengths`: in each pair of sequences 2i, 2i + 1 one of the two, drawn from the seed, has length 1024; positions at or past a sequence's length are padding.
All inputs are finite; a program needn't handle non-finite values.
Results may differ from a plain program's by a relative error of at most 0.024.
Values may be sent and summed in bfloat16 or wider, within the bound.
A program may use at most 192 MiB of HBM per device.

v0:
```python
import math

import jax
import jax.numpy as jnp
from jax import lax
from jax.sharding import PartitionSpec as P

HEADS = 8
HEAD_DIM = 64


def smooth(value):
    return jax.nn.gelu(value, approximate=True)


def project(left, right):
    return jnp.dot(left, right, preferred_element_type=jnp.float32)


def per_device(
    tokens,
    lengths,
    w_query,
    w_key,
    w_value,
    w_out,
    w_in,
    b_in,
    w_back,
    b_back,
    alpha_attn,
    alpha_ffn,
    cotangent,
):
    seq_count, block_len, width = tokens.shape
    rows_total = seq_count * block_len
    inputs = tokens.reshape(rows_total, width)
    own_start = lax.axis_index("blk") * block_len
    query_pos = own_start + jnp.arange(block_len, dtype=jnp.int32)
    query_live = (query_pos[None, :] < lengths[:, None]).astype(jnp.float32).reshape(rows_total, 1)
    query_bf = project(inputs, w_query).astype(jnp.bfloat16)
    key_bf = project(inputs, w_key).astype(jnp.bfloat16).reshape(seq_count, block_len, width)
    value_bf = project(inputs, w_value).astype(jnp.bfloat16).reshape(seq_count, block_len, width)
    query_heads = query_bf.reshape(seq_count, block_len, HEADS, HEAD_DIM)

    def pair_mask(row_pos, col_pos):
        causal = col_pos[None, None, :] <= row_pos[None, :, None]
        inside = col_pos[None, None, :] < lengths[:, None, None]
        return causal & inside

    initial = (
        jnp.full((seq_count, HEADS, block_len), -1e30, jnp.float32),
        jnp.zeros((seq_count, HEADS, block_len), jnp.float32),
        jnp.zeros((seq_count, HEADS, block_len, HEAD_DIM), jnp.float32),
    )
    key_piece = lax.all_gather(key_bf, "blk", axis=1, tiled=True)
    value_piece = lax.all_gather(value_bf, "blk", axis=1, tiled=True)
    span = key_piece.shape[1]
    fold_step_len = math.gcd(span, 512)

    def one_step(state, block_index):
        run_max, run_sum, run_acc = state
        begin = block_index * fold_step_len
        key_block = lax.dynamic_slice_in_dim(key_piece, begin, fold_step_len, 1).reshape(
            seq_count, fold_step_len, HEADS, HEAD_DIM
        )
        value_block = lax.dynamic_slice_in_dim(value_piece, begin, fold_step_len, 1).reshape(
            seq_count, fold_step_len, HEADS, HEAD_DIM
        )
        allowed = pair_mask(query_pos, begin + jnp.arange(fold_step_len, dtype=jnp.int32))[:, None]
        scores = (
            jnp.einsum(
                "sqhe,skhe->shqk", query_heads, key_block, preferred_element_type=jnp.float32
            )
            * 0.125
        )
        scores = jnp.where(allowed, scores, -1e30)
        new_max = jnp.maximum(run_max, jnp.max(scores, axis=-1))
        weights = jnp.where(allowed, jnp.exp(scores - new_max[..., None]), 0.0)
        factor = jnp.exp(run_max - new_max)
        run_sum = run_sum * factor + jnp.sum(weights, axis=-1)
        update = jnp.einsum(
            "shqk,skhe->shqe",
            weights.astype(jnp.bfloat16),
            value_block,
            preferred_element_type=jnp.float32,
        )
        run_acc = run_acc * factor[..., None] + update
        return ((new_max, run_sum, run_acc), None)

    result, unused = lax.scan(one_step, initial, jnp.arange(span // fold_step_len, dtype=jnp.int32))
    state = result
    run_max, run_sum, run_acc = state
    log_total = run_max + jnp.log(run_sum)
    attn_heads = jnp.transpose(run_acc / run_sum[..., None], (0, 2, 1, 3))
    attn_rows = attn_heads.reshape(rows_total, width)
    attn_bf = attn_rows.astype(jnp.bfloat16)
    branch = project(attn_bf, w_out)
    resid = inputs.astype(jnp.float32) + alpha_attn * query_live * branch
    resid_bf = resid.astype(jnp.bfloat16)
    hidden = project(resid_bf, w_in) + b_in
    activated, gelu_pull = jax.vjp(smooth, hidden)
    act_bf = activated.astype(jnp.bfloat16)
    ffn_out = project(act_bf, w_back) + b_back
    outputs = (resid + alpha_ffn * ffn_out).astype(jnp.bfloat16)
    grad_out = cotangent.reshape(rows_total, width).astype(jnp.float32)
    grad_alpha_ffn = jnp.sum(grad_out * ffn_out)
    grad_ffn_bf = (alpha_ffn * grad_out).astype(jnp.bfloat16)
    grad_b_back = jnp.sum(grad_ffn_bf.astype(jnp.float32), axis=0)
    grad_w_back = project(act_bf.T, grad_ffn_bf)
    grad_act = project(grad_ffn_bf, w_back.T)
    (grad_hidden,) = gelu_pull(grad_act)
    grad_hidden_bf = grad_hidden.astype(jnp.bfloat16)
    grad_b_in = jnp.sum(grad_hidden_bf.astype(jnp.float32), axis=0)
    grad_w_in = project(resid_bf.T, grad_hidden_bf)
    grad_resid = grad_out + project(grad_hidden_bf, w_in.T)
    grad_alpha_attn = jnp.sum(grad_resid * query_live * branch)
    grad_branch_bf = (alpha_attn * query_live * grad_resid).astype(jnp.bfloat16)
    grad_w_out = project(attn_bf.T, grad_branch_bf)
    grad_attn_bf = project(grad_branch_bf, w_out.T).astype(jnp.bfloat16)
    grad_attn_heads = grad_attn_bf.reshape(seq_count, block_len, HEADS, HEAD_DIM)
    delta = jnp.sum(grad_attn_heads.astype(jnp.float32) * attn_heads, axis=-1).transpose(0, 2, 1)
    gathered = (
        lax.all_gather(key_bf, "blk", axis=1, tiled=True),
        lax.all_gather(value_bf, "blk", axis=1, tiled=True),
    )
    key_all, value_all = gathered
    full_len = key_all.shape[1]
    step_len = math.gcd(full_len, 512)

    def back_step(state_now, block_index):
        grad_query, grad_keys, grad_values = state_now
        begin = block_index * step_len
        key_block = lax.dynamic_slice_in_dim(key_all, begin, step_len, 1).reshape(
            seq_count, step_len, HEADS, HEAD_DIM
        )
        value_block = lax.dynamic_slice_in_dim(value_all, begin, step_len, 1).reshape(
            seq_count, step_len, HEADS, HEAD_DIM
        )
        allowed = pair_mask(query_pos, begin + jnp.arange(step_len, dtype=jnp.int32))[:, None]
        scores = (
            jnp.einsum(
                "sqhe,skhe->shqk", query_heads, key_block, preferred_element_type=jnp.float32
            )
            * 0.125
        )
        probs = jnp.where(allowed, jnp.exp(scores - log_total[..., None]), 0.0)
        grad_probs = jnp.einsum(
            "sqhe,skhe->shqk", grad_attn_heads, value_block, preferred_element_type=jnp.float32
        )
        grad_scores = (0.125 * (probs * (grad_probs - delta[..., None]))).astype(jnp.bfloat16)
        grad_query = grad_query + jnp.einsum(
            "shqk,skhe->sqhe", grad_scores, key_block, preferred_element_type=jnp.float32
        )
        grad_values_block = jnp.einsum(
            "shqk,sqhe->skhe",
            probs.astype(jnp.bfloat16),
            grad_attn_heads,
            preferred_element_type=jnp.float32,
        )
        grad_keys_block = jnp.einsum(
            "shqk,sqhe->skhe", grad_scores, query_heads, preferred_element_type=jnp.float32
        )
        grad_keys = lax.dynamic_update_slice_in_dim(
            grad_keys, grad_keys_block.reshape(seq_count, step_len, width), begin, 1
        )
        grad_values = lax.dynamic_update_slice_in_dim(
            grad_values, grad_values_block.reshape(seq_count, step_len, width), begin, 1
        )
        return ((grad_query, grad_keys, grad_values), None)

    query_zero = jnp.zeros((seq_count, block_len, HEADS, HEAD_DIM), jnp.float32)
    block_steps = jnp.arange(full_len // step_len, dtype=jnp.int32)
    back_start = (
        query_zero,
        jnp.zeros((seq_count, full_len, width), jnp.float32),
        jnp.zeros((seq_count, full_len, width), jnp.float32),
    )
    back_state, unused = lax.scan(back_step, back_start, block_steps)
    grad_query_all, grad_keys_all, grad_values_all = back_state
    key_sum, value_sum = (
        lax.psum_scatter(
            grad_keys_all.astype(jnp.bfloat16), "blk", scatter_dimension=1, tiled=True
        ).astype(jnp.float32),
        lax.psum_scatter(
            grad_values_all.astype(jnp.bfloat16), "blk", scatter_dimension=1, tiled=True
        ).astype(jnp.float32),
    )
    grad_query_bf = grad_query_all.reshape(rows_total, width).astype(jnp.bfloat16)
    grad_key_bf = key_sum.reshape(rows_total, width).astype(jnp.bfloat16)
    grad_value_bf = value_sum.reshape(rows_total, width).astype(jnp.bfloat16)
    grad_w_query = project(inputs.T, grad_query_bf)
    grad_w_key = project(inputs.T, grad_key_bf)
    grad_w_value = project(inputs.T, grad_value_bf)
    grad_input = (
        grad_resid
        + project(grad_query_bf, w_query.T)
        + project(grad_key_bf, w_key.T)
        + project(grad_value_bf, w_value.T)
    )
    grad_input = grad_input.astype(jnp.bfloat16).reshape(seq_count, block_len, width)
    totals = lax.psum(
        (
            grad_w_query,
            grad_w_key,
            grad_w_value,
            grad_w_out,
            grad_w_in,
            grad_b_in,
            grad_w_back,
            grad_b_back,
            grad_alpha_attn,
            grad_alpha_ffn,
        ),
        ("batch", "blk"),
    )
    (
        sum_query,
        sum_key,
        sum_value,
        sum_out,
        sum_in,
        sum_b_in,
        sum_back,
        sum_b_back,
        sum_alpha_attn,
        sum_alpha_ffn,
    ) = totals
    return (
        outputs.reshape(seq_count, block_len, width),
        grad_input,
        sum_query,
        sum_key,
        sum_value,
        sum_out,
        sum_in,
        sum_b_in,
        sum_back,
        sum_b_back,
        sum_alpha_attn,
        sum_alpha_ffn,
    )


def solution(mesh):
    return jax.shard_map(
        per_device,
        mesh=mesh,
        in_specs=(
            P("batch", "blk", None),
            P("batch"),
            P(),
            P(),
            P(),
            P(),
            P(),
            P(),
            P(),
            P(),
            P(),
            P(),
            P("batch", "blk", None),
        ),
        out_specs=(
            P("batch", "blk", None),
            P("batch", "blk", None),
            P(),
            P(),
            P(),
            P(),
            P(),
            P(),
            P(),
            P(),
            P(),
            P(),
        ),
        check_vma=False,
    )
```

profile of v0, /device:TPU:0, one launch (start us, length us, event | category | flops | bytes accessed | tf_op | source)
XLA Modules:
  0.0 587.1 jit_solution(433714965193956545)
XLA Ops:
  19.1 2.0 fusion.37
  21.1 38.0 %all-gather.3.cloned.1.call-done = bf16[2,1024,512]{1,2,0:T(8,128)(2,1)} async-done(((bf16[2,256,512]{1,2,0:T(8,128)(2,1)}), bf16[2,1024,512]{1,2,0:T(8,128)(2,1)}) %all-gather.3.cloned.1.call-update) | async-done | bytes 2097168 | tf_op jit(solution)/shard_map/all_gather | solution.py:56
  59.2 46.6 %all-gather.5.cloned.1.call-done = bf16[2,1024,512]{1,2,0:T(8,128)(2,1)} async-done(((bf16[2,256,512]{1,2,0:T(8,128)(2,1)}), bf16[2,1024,512]{1,2,0:T(8,128)(2,1)}) %all-gather.5.cloned.1.call-update) | async-done | bytes 2097168 | tf_op jit(solution)/shard_map/all_gather | solution.py:57
  105.8 39.1 %while.30 = (s32[]{:T(128)}, f32[2,8,256]{2,1,0:T(8,128)S(1)}, f32[2,8,256]{2,1,0:T(8,128)S(1)}, f32[2,8,256,64]{2,3,1,0:T(8,128)}, s32[2]{0:T(128)S(1)}, /*inde...) while((s32[]{:T(128)}, f32[2,8,256]{2,1,0:T(8,128)S(1)}, ...), condition=%wide.region_3.4_spmd.clone, body=%wide.region_0.3_spmd.clone.sunk | while | flops 565335808 | bytes 69216512 | solution.py:91
  107.5 2.7 constant_dynamic-slice_fusion.7
  110.2 4.8 fusion.121
  115.0 5.1 fusion.122
  120.8 4.4 fusion.124
  126.9 2.7 constant_dynamic-slice_fusion.7
  129.5 4.8 fusion.121
  134.4 5.1 fusion.122
  140.2 4.7 fusion.124
  144.9 3.4 bitcast_convert_fusion
  148.5 2.7 fusion.40
  153.3 4.0 convert_reduce_fusion
  167.9 65.3 %while.31 = (s32[]{:T(128)}, f32[2,256,8,64]{1,3,2,0:T(8,128)}, bf16[2,1024,512]{2,1,0:T(8,128)(2,1)}, bf16[2,1024,512]{2,1,0:T(8,128)(2,1)}, s32[2]{0:T(128)S(1...) while((s32[]{:T(128)}, f32[2,256,8,64]{1,3,2,0:T(8,128)}, ...), condition=%wide.region_6.7_spmd.clone, body=%wide.region_5.6_spmd.clone.sunk | while | flops 1366165248 | bytes 111208880 | solution.py:179
  170.6 2.5 fusion.135
  173.7 4.5 fusion.136
  178.2 4.0 fusion.137
  182.2 6.2 %fusion.138 = bf16[2,8,512,64]{2,3,1,0:T(8,128)(2,1)} fusion(bf16[2,256,8,64]{1,3,2,0:T(8,128)(2,1)S(1)} %copy-done.27, f32[2,8,512,256]{3,2,1,0:T(8,128)} %copy-done.2, f32[2,8,256]{2,1,0:T(8,128)S(1)} %get-tuple-element.640, pred[2,256,512]{1,2,0:T(8,128)(4,1)S(1)} %broadcast_and_fusion.5), kind=kOutput, calls=%fused_computation.30.clone.1 | convolution fusion | flops 276824064 | bytes 10240000 | tf_op jit(solution)/shard_map/while/body/eval_jaxpr/shqk,sqhe->skhe/dot_general | solution.py:155
  188.4 2.3 copy.106
  190.6 4.5 fusion.139
  195.2 2.3 copy.107
  197.5 3.0 constant_dynamic-update-slice_fusion.3
  203.1 2.5 fusion.135
  206.2 4.5 fusion.136
  210.7 4.3 fusion.137
  215.0 6.2 %fusion.138 = bf16[2,8,512,64]{2,3,1,0:T(8,128)(2,1)} fusion(bf16[2,256,8,64]{1,3,2,0:T(8,128)(2,1)S(1)} %copy-done.27, f32[2,8,512,256]{3,2,1,0:T(8,128)} %copy-done.2, f32[2,8,256]{2,1,0:T(8,128)S(1)} %get-tuple-element.640, pred[2,256,512]{1,2,0:T(8,128)(4,1)S(1)} %broadcast_and_fusion.5), kind=kOutput, calls=%fused_computation.30.clone.1 | convolution fusion | flops 276824064 | bytes 10240000 | tf_op jit(solution)/shard_map/while/body/eval_jaxpr/shqk,sqhe->skhe/dot_general | solution.py:155
  221.1 2.3 copy.106
  223.4 4.5 fusion.139
  228.0 2.3 copy.107
  230.2 3.0 constant_dynamic-update-slice_fusion.3
  235.2 2.6 convolution_bitcast_fusion.3
  239.4 3.3 fusion.49
  242.7 4.0 fusion.44
  246.7 28.7 %reduce-scatter.3.cloned.1.call-done = bf16[2,256,512]{2,1,0:T(8,128)(2,1)} async-done(((bf16[2,1024,512]{2,1,0:T(8,128)(2,1)}), bf16[2,256,512]{2,1,0:T(8,128)(2,1)}) %reduce-scatter.3.cloned.1.call-update) | async-done | bytes 524304 | tf_op jit(solution)/shard_map/reduce_scatter | solution.py:182
  275.4 2.5 convolution_bitcast_fusion.2
  277.9 43.1 %reduce-scatter.5.cloned.1.call-done = bf16[2,256,512]{2,1,0:T(8,128)(2,1)} async-done(((bf16[2,1024,512]{2,1,0:T(8,128)(2,1)}), bf16[2,256,512]{2,1,0:T(8,128)(2,1)}) %reduce-scatter.5.cloned.1.call-update) | async-done | bytes 524304 | tf_op jit(solution)/shard_map/reduce_scatter | solution.py:185
  321.0 2.5 convolution_bitcast_fusion.1
  325.4 6.3 %fusion.38 = (f32[]{:T(128)}, bf16[512,512]{1,0:T(8,128)(2,1)}, f32[]{:T(128)}) fusion(bf16[2,256,512]{2,1,0:T(8,128)(2,1)} %param.29, f32[]{:T(128)S(6)} %copy.141, f32[512,512]{1,0:T(8,128)} %get-tuple-element.399, f32[512]{0:T(512)S(1)} %bitcast.218, bf16[2,256,512]{2,1,0:T(8,128)(2,1)S(1)} %copy-done.8, f32[512,512]{1,0:T(8,128)} %copy-done.9, ...), kind=kOutput, calls=%fused_computation.75 | convolution fusion | flops 1087635456 | bytes 9975820 | tf_op jit(solution)/shard_map/dot_general | solution.py:17
  331.7 41.2 %all-reduce = (f32[2048]{0:T(1024)}, f32[512]{0:T(512)}, f32[]{:T(128)}, f32[]{:T(128)}) all-reduce(f32[2048]{0:T(1024)S(1)} %get-tuple-element.385, f32[512]{0:T(512)S(1)} %convert_reduce_fusion.1, f32[]{:T(128)} %get-tuple-element.397, f32[]{:T(128)} %get-tuple-element.395), channel_id=1, replica_groups=mesh['batch'=8,'blk'=4] {'batch','blk'}, use_global_device_ids=true, to_apply=%region_15.16 | all-reduce | flops 2562 | bytes 20496 | tf_op jit(solution)/shard_map/psum | solution.py:202
  372.9 2.0 convolution_add_fusion.2
  377.9 187.1 %all-reduce.4.cloned.1.call-done = (f32[512,512]{0,1:T(8,128)}, f32[512,512]{0,1:T(8,128)}, f32[512,512]{0,1:T(8,128)}, f32[512,512]{1,0:T(8,128)}, f32[512,2048]{1,0:T(8,128)}, /*index=5*/f32[2048,512]{1,0:T(8,128)}) async-done(((f32[512,512]{0,1:T(8,128)}, f32[512,512]{0,1:T(8,128)}, f32[512,512]{0,1:T(8,128)}, f32[512,512]{1,0:T(8,128)}, f32[512,2048]{1,0:T(8,128)}, /*index=5*/f32[2048,512]{1,0:T(8,128)}), ...) | async-done | bytes 12582928 | tf_op jit(solution)/shard_map/psum | solution.py:202
  565.0 2.6 copy.78
  567.6 2.5 copy.79
  570.2 2.5 copy.80
  573.7 4.8 copy.143
  578.5 2.0 copy.144
  (167 shorter events, 41.2 us)
Async XLA Ops:
  7.2 146.0 %copy-start = (bf16[2048,512]{1,0:T(8,128)(2,1)S(1)}, bf16[2048,512]{1,0:T(8,128)(2,1)}, u32[]{:S(2)}) copy-start(bf16[2048,512]{1,0:T(8,128)(2,1)} %param.25) | copy-start | bytes 6291460
  7.2 7.2 %copy-start.7 = (bf16[2,256,512]{2,1,0:T(8,128)(2,1)S(1)}, bf16[2,256,512]{2,1,0:T(8,128)(2,1)}, u32[]{:S(2)}) copy-start(bf16[2,256,512]{2,1,0:T(8,128)(2,1)} %param.17) | copy-start | bytes 1572868
  7.2 7.1 %copy-start.30 = (s32[2]{0:T(128)S(1)}, s32[2]{0:T(128)}, u32[]{:S(2)}) copy-start(s32[2]{0:T(128)} %param.18) | copy-start | bytes 28
  7.2 52.0 %all-gather.3.cloned.1.call-start = ((), (), s32[]{:S(2)}) async-start(), calls=%async_computation.2 | async-start | bytes 2621440 | tf_op jit(solution)/shard_map/all_gather | solution.py:56
  10.1 95.7 %all-gather.5.cloned.1.call-start = ((), (), s32[]{:S(2)}) async-start(), calls=%async_computation.3 | async-start | bytes 2621440 | tf_op jit(solution)/shard_map/all_gather | solution.py:57
  12.9 262.5 %reduce-scatter.3.cloned.1.call-start = ((), (), s32[]{:S(2)}) async-start(), calls=%async_computation.4 | async-start | bytes 2621440 | tf_op jit(solution)/shard_map/reduce_scatter | solution.py:182
  14.3 91.5 %copy-start.31 = (s32[256]{0:T(256)}, s32[256]{0:T(256)S(1)}, u32[]{:S(2)}) copy-start(s32[256]{0:T(256)S(1)} %iota_add_fusion.4) | copy-start | bytes 3076
  115.0 5.8 copy-start.1
  134.4 5.8 copy-start.1
  144.9 7.0 %copy-start.19 = (bf16[512,2048]{1,0:T(8,128)(2,1)S(1)}, bf16[512,2048]{1,0:T(8,128)(2,1)}, u32[]{:S(2)}) copy-start(bf16[512,2048]{1,0:T(8,128)(2,1)} %param.23) | copy-start | bytes 6291460
  148.4 2.7 copy-start.11
  151.1 0.8 copy-start.13
  151.1 2.1 copy-start.28
  151.1 2.1 copy-start.33
  153.2 4.0 copy-start.16
  153.3 4.0 copy-start.23
  157.3 1.4 copy-start.20
  157.3 2.3 copy-start.22
  158.7 1.0 copy-start.9
  167.9 1.3 copy-start.3
  170.6 3.0 copy-start.5
  170.6 3.1 copy-start.26
  173.1 5.1 copy-start.2
  178.2 4.0 copy-start.27
  182.2 8.5 %copy-start.4 = (bf16[2,256,8,64]{1,3,2,0:T(8,128)(2,1)S(1)}, bf16[2,256,8,64]{1,3,2,0:T(8,128)(2,1)}, u32[]{:S(2)}) copy-start(bf16[2,256,8,64]{1,3,2,0:T(8,128)(2,1)} %copy-done.3) | copy-start | bytes 1572868 | tf_op jit(solution)/shard_map/while
  200.4 1.3 copy-start.3
  203.1 3.0 copy-start.5
  203.1 3.1 copy-start.26
  205.6 5.1 copy-start.2
  210.7 4.3 copy-start.27
  215.0 8.5 %copy-start.4 = (bf16[2,256,8,64]{1,3,2,0:T(8,128)(2,1)S(1)}, bf16[2,256,8,64]{1,3,2,0:T(8,128)(2,1)}, u32[]{:S(2)}) copy-start(bf16[2,256,8,64]{1,3,2,0:T(8,128)(2,1)} %copy-done.3) | copy-start | bytes 1572868 | tf_op jit(solution)/shard_map/while
  233.2 1.2 copy-start.6
  233.3 87.7 %reduce-scatter.5.cloned.1.call-start = ((), (), s32[]{:S(2)}) async-start(), calls=%async_computation.5 | async-start | bytes 2621440 | tf_op jit(solution)/shard_map/reduce_scatter | solution.py:185
  233.8 331.2 %all-reduce.4.cloned.1.call-start = ((), (), s32[]{:S(2)}) async-start(), calls=%async_computation.6 | async-start | bytes 25165824 | tf_op jit(solution)/shard_map/psum | solution.py:202
  234.1 3.7 copy-start.10
  234.1 3.7 copy-start.12
  234.5 4.9 copy-start.14
  234.5 4.9 copy-start.21
  237.8 4.8 copy-start.17
  237.8 4.8 copy-start.29
  242.7 32.8 %copy-start.8 = (bf16[2,256,512]{2,1,0:T(8,128)(2,1)S(1)}, bf16[2,256,512]{2,1,0:T(8,128)(2,1)}, u32[]{:S(2)}) copy-start(bf16[2,256,512]{2,1,0:T(8,128)(2,1)} %param.17) | copy-start | bytes 1572868
  323.4 0.7 copy-start.32
  323.4 1.9 copy-start.34
  331.7 44.9 %copy-start.18 = (bf16[512,512]{1,0:T(8,128)(2,1)S(1)}, bf16[512,512]{1,0:T(8,128)(2,1)}, u32[]{:S(2)}) copy-start(bf16[512,512]{1,0:T(8,128)(2,1)} %param.21) | copy-start | bytes 1572868
  372.9 3.7 copy-start.24
  565.0 7.7 %copy-start.25 = (f32[512,512]{1,0:T(8,128)S(1)}, f32[512,512]{1,0:T(8,128)}, u32[]{:S(2)}) copy-start(f32[512,512]{1,0:T(8,128)} %get-tuple-element.654) | copy-start | bytes 3145732
  573.7 4.9 copy-start.15
Sparse Core Ops, SparseCore 0:
  10.2 48.9 all-gather.2
  61.3 44.4 all-gather.4
  233.4 41.9 reduce-scatter.2
  277.7 43.2 reduce-scatter.4
  327.8 237.1 all-reduce.3
where the time goes:
time: 588 us; the launch traced here: 587 us
  waiting for transfers between devices  344 us (59%)
  matrix products  105 us (18%)
  local copies, waits for them, and re-layouts  57.6 us (10%)
  blocking collectives  41.2 us (7%)
  other arithmetic  20.5 us (3%)
  between operations  15.5 us (3%)
    psum x1, waiting for transfers between devices, per_device(): lax.psum((grad_w_query, grad_w_key, grad_w_value, grad_w_out, grad_w_in,...  187 us
    all_gather x1, waiting for transfers between devices, per_device(): value_piece = lax.all_gather(value_bf, 'blk', axis=1, tiled=True)  46.6 us
    reduce_scatter x1, waiting for transfers between devices, per_device(): lax.psum_scatter(grad_values_all.astype(jnp.bfloat16), 'blk', scatter_dim...  43.1 us
    dot_general x18, matrix products, project(): return jnp.dot(left, right, preferred_element_type=jnp.float32)  42.4 us
    psum x1, blocking collectives, per_device(): lax.psum((grad_w_query, grad_w_key, grad_w_value, grad_w_out, grad_w_in,...  41.2 us
    all_gather x1, waiting for transfers between devices, per_device(): key_piece = lax.all_gather(key_bf, 'blk', axis=1, tiled=True)  38 us
    reduce_scatter x1, waiting for transfers between devices, per_device(): lax.psum_scatter(grad_keys_all.astype(jnp.bfloat16), 'blk', scatter_dimen...  28.7 us
    unnamed x69, local copies, waits for them, and re-layouts  21.2 us
  transfers between devices with their start and end apart: 5, of which 5 were waited for; matrix products, arithmetic and copies ran while one was open for 6% of the time, Pallas kernels for 0%

commit v1 on v0

--- a/solution.py
+++ b/solution.py
@@ -1,12 +1,228 @@
+import functools
 import math
 
 import jax
 import jax.numpy as jnp
 from jax import lax
+from jax.experimental import pallas as pl
+from jax.experimental.pallas import tpu as pltpu
 from jax.sharding import PartitionSpec as P
 
 HEADS = 8
 HEAD_DIM = 64
+
+
+MESH = pl.DeviceIdType.MESH
+CHUNK_ROWS = 1024
+
+
+class Reducer:
+    def __init__(self, nb, nz, rows):
+        self.rows = rows
+        plane = [("batch", 1 << i) for i in range(1, nb.bit_length() - 1)]
+        line = [("blk", 1 << i) for i in range(nz.bit_length() - 1)]
+        self.orders = [plane + line, plane[::-1] + line]
+        self.all_bits = [("batch", 1)] + plane + line
+        self.steps = len(self.orders[0])
+        self.halves = 0
+        length, land = rows // 4, rows // 2
+        self.sizes, self.lands = [], [[], []]
+        for _ in range(self.steps):
+            if length >= 32:
+                length //= 2
+                self.halves += 1
+            self.sizes.append(length)
+            for o in (0, 1):
+                self.lands[o].append(land)
+                land += length
+        self.land_rows = land
+        self.sems = 2 + 4 * self.steps
+
+    def scratch(self, chunks, width):
+        return [
+            pltpu.VMEM((chunks, self.land_rows, width), jnp.bfloat16),
+            pltpu.SemaphoreType.DMA((chunks, self.sems)),
+            pltpu.SemaphoreType.DMA((chunks, self.sems)),
+        ]
+
+    def bind(self, grads, total, land, send_sem, recv_sem):
+        self.grads, self.total, self.land = grads, total, land
+        self.send_sem, self.recv_sem = send_sem, recv_sem
+        self.at = {"batch": lax.axis_index("batch"), "blk": lax.axis_index("blk")}
+        core = self.at["batch"] % 2
+        half = self.rows // 2
+        self.core_keep, self.core_send = core * half, (1 - core) * half
+        self.keep, self.send, self.own = [[], []], [[], []], []
+        for o in (0, 1):
+            off = self.core_keep + o * (half // 2)
+            for i, (axis, bit) in enumerate(self.orders[o]):
+                mine = (self.at[axis] // bit) % 2
+                if i < self.halves:
+                    self.keep[o].append(off + mine * self.sizes[i])
+                    self.send[o].append(off + (1 - mine) * self.sizes[i])
+                    off = self.keep[o][-1]
+                else:
+                    self.keep[o].append(off)
+                    self.send[o].append(off)
+            self.own.append(off)
+
+    def partner(self, axis, bit):
+        mine = (self.at[axis] // bit) % 2
+        there = self.at[axis] + bit * (1 - 2 * mine)
+        if axis == "batch":
+            return (there, self.at["blk"])
+        return (self.at["batch"], there)
+
+    def copy(self, c, src, src_row, dst, dst_row, size, sem, axis, bit):
+        return pltpu.make_async_remote_copy(
+            src_ref=src.at[c, pl.ds(pl.multiple_of(src_row, 16), size)],
+            dst_ref=dst.at[c, pl.ds(pl.multiple_of(dst_row, 16), size)],
+            send_sem=self.send_sem.at[c, sem],
+            recv_sem=self.recv_sem.at[c, sem],
+            device_id=self.partner(axis, bit),
+            device_id_type=MESH,
+        )
+
+    def core_out(self, c):
+        return self.copy(c, self.grads, self.core_send, self.land, 0, self.rows // 2, 0, "batch", 1)
+
+    def core_back(self, c):
+        return self.copy(
+            c, self.total, self.core_keep, self.total, self.core_keep, self.rows // 2, 1, "batch", 1
+        )
+
+    def out(self, c, o, i):
+        axis, bit = self.orders[o][i]
+        return self.copy(
+            c, self.grads, self.send[o][i], self.land, self.lands[o][i], self.sizes[i],
+            2 + o * self.steps + i, axis, bit,
+        )
+
+    def back(self, c, o, i):
+        axis, bit = self.orders[o][i]
+        row = self.keep[o][i]
+        return self.copy(
+            c, self.total, row, self.total, row, self.sizes[i],
+            2 + (2 + o) * self.steps + i, axis, bit,
+        )
+
+    def add(self, c, row, land_row, size, last=False):
+        piece = min(size, 64)
+        target = self.total if last else self.grads
+
+        def body(k, carry):
+            here = pl.ds(pl.multiple_of(row + k * piece, 16), piece)
+            there = pl.ds(pl.multiple_of(land_row + k * piece, 16), piece)
+            target[c, here] = self.grads[c, here] + self.land[c, there]
+            return carry
+
+        lax.fori_loop(0, size // piece, body, 0)
+
+    def stages(self):
+        return 2 * self.steps + 3 - (self.steps - self.halves)
+
+    def stage(self, k, c):
+        n = self.steps
+        if k == 0:
+            self.core_out(c).start()
+        elif k <= n + 1:
+            i = k - 2
+            if k == 1:
+                self.core_out(c).wait()
+                self.add(c, self.core_keep, 0, self.rows // 2)
+            else:
+                for o in (0, 1):
+                    self.out(c, o, i).wait()
+                    self.add(c, self.keep[o][i], self.lands[o][i], self.sizes[i], i == n - 1)
+            if i + 1 < n:
+                for o in (0, 1):
+                    self.out(c, o, i + 1).start()
+            else:
+                for o in (0, 1):
+                    self.back(c, o, self.halves - 1).start()
+        elif k < self.stages() - 1:
+            i = self.halves - 1 - (k - n - 2)
+            for o in (0, 1):
+                self.back(c, o, i).wait()
+            if i > 0:
+                for o in (0, 1):
+                    self.back(c, o, i - 1).start()
+            else:
+                self.core_back(c).start()
+        else:
+            self.core_back(c).wait()
+
+    def small_copy(self, small, land, send_sem, recv_sem, i):
+        axis, bit = self.all_bits[i]
+        return pltpu.make_async_remote_copy(
+            src_ref=small.at[i],
+            dst_ref=land.at[i],
+            send_sem=send_sem.at[i],
+            recv_sem=recv_sem.at[i],
+            device_id=self.partner(axis, bit),
+            device_id_type=MESH,
+        )
+
+
+def reduce_kernel(
+    plan, chunks, grads_in, small_in, total, small_out,
+    grads, land, send_sem, recv_sem, small, small_land, small_send, small_recv, load_sem,
+):
+    plan.bind(grads, total, land, send_sem, recv_sem)
+    load = pltpu.make_async_copy(grads_in, grads, load_sem)
+    load.start()
+    barrier = pltpu.get_barrier_semaphore()
+    for axis, bit in plan.all_bits:
+        pl.semaphore_signal(barrier, inc=1, device_id=plan.partner(axis, bit), device_id_type=MESH)
+    pl.semaphore_wait(barrier, len(plan.all_bits))
+    small[0] = small_in[...]
+    load.wait()
+
+    def tick(t, carry):
+        for k in range(plan.stages() - 1, -1, -1):
+            c = t - k
+
+            @pl.when((c >= 0) & (c < chunks))
+            def _():
+                plan.stage(k, c)
+
+        return carry
+
+    lax.fori_loop(0, chunks + plan.stages() - 1, tick, 0)
+    steps = len(plan.all_bits)
+    for i in range(steps):
+        plan.small_copy(small, small_land, small_send, small_recv, i).start()
+        plan.small_copy(small, small_land, small_send, small_recv, i).wait()
+        small[i + 1] = small[i] + small_land[i]
+    small_out[...] = small[steps]
+
+
+def reduce_all(grads, small, nb, nz):
+    chunks, rows, width = grads.shape
+    plan = Reducer(nb, nz, rows)
+    steps = len(plan.all_bits)
+    return pl.pallas_call(
+        functools.partial(reduce_kernel, plan, chunks),
+        out_shape=(
+            jax.ShapeDtypeStruct(grads.shape, jnp.bfloat16),
+            jax.ShapeDtypeStruct(small.shape, jnp.float32),
+        ),
+        in_specs=[pl.BlockSpec(memory_space=pl.ANY), pl.BlockSpec(memory_space=pltpu.VMEM)],
+        out_specs=(pl.BlockSpec(memory_space=pltpu.VMEM), pl.BlockSpec(memory_space=pltpu.VMEM)),
+        scratch_shapes=[pltpu.VMEM(grads.shape, jnp.bfloat16)]
+        + plan.scratch(chunks, width)
+        + [
+            pltpu.VMEM((steps + 1,) + small.shape, jnp.float32),
+            pltpu.VMEM((steps,) + small.shape, jnp.float32),
+            pltpu.SemaphoreType.DMA((steps,)),
+            pltpu.SemaphoreType.DMA((steps,)),
+            pltpu.SemaphoreType.DMA,
+        ],
+        name="grad_sum",
+        compiler_params=pltpu.CompilerParams(
+            collective_id=0, has_side_effects=True, vmem_limit_bytes=48 << 20
+        ),
+    )(grads, small)
 
 
 def smooth(value):
@@ -199,33 +415,33 @@
         + project(grad_value_bf, w_value.T)
     )
     grad_input = grad_input.astype(jnp.bfloat16).reshape(seq_count, block_len, width)
-    totals = lax.psum(
-        (
-            grad_w_query,
-            grad_w_key,
-            grad_w_value,
-            grad_w_out,
-            grad_w_in,
-            grad_b_in,
-            grad_w_back,
-            grad_b_back,
-            grad_alpha_attn,
-            grad_alpha_ffn,
-        ),
-        ("batch", "blk"),
-    )
-    (
-        sum_query,
-        sum_key,
-        sum_value,
-        sum_out,
-        sum_in,
-        sum_b_in,
-        sum_back,
-        sum_b_back,
-        sum_alpha_attn,
-        sum_alpha_ffn,
-    ) = totals
+    nb, nz = lax.axis_size("batch"), lax.axis_size("blk")
+    ff = grad_w_back.shape[0]
+    pieces = [grad_w_query, grad_w_key, grad_w_value, grad_w_out]
+    pieces += [grad_w_in[:, k * width : (k + 1) * width] for k in range(ff // width)]
+    pieces += [grad_w_back]
+    packed = jnp.concatenate([p.astype(jnp.bfloat16) for p in pieces], axis=0)
+    packed = packed.reshape(-1, CHUNK_ROWS, width)
+    small = jnp.concatenate(
+        [
+            grad_b_in.reshape(-1, width),
+            grad_b_back.reshape(1, width),
+            jnp.full((1, width), grad_alpha_attn),
+            jnp.full((1, width), grad_alpha_ffn),
+            jnp.zeros((1, width), jnp.float32),
+        ],
+        axis=0,
+    )
+    total, small_sum = reduce_all(packed, small, nb, nz)
+    flat = total.reshape(-1, width).astype(jnp.float32)
+    sum_query, sum_key, sum_value, sum_out = [flat[k * width : (k + 1) * width] for k in range(4)]
+    sum_in = jnp.concatenate([flat[(4 + k) * width : (5 + k) * width] for k in range(ff // width)], axis=1)
+    sum_back = flat[4 * width + ff :]
+    rows_b = ff // width
+    sum_b_in = small_sum[:rows_b].reshape(ff)
+    sum_b_back = small_sum[rows_b]
+    sum_alpha_attn = small_sum[rows_b + 1, 0]
+    sum_alpha_ffn = small_sum[rows_b + 2, 0]
     return (
         outputs.reshape(seq_count, block_len, width),
         grad_input,

time: 588 us -> 458 us (0.78)
  waiting for transfers between devices: 344 us -> 151 us
  Pallas kernels: 0 us -> 95.5 us
  blocking collectives: 41.2 us -> 0 us
  other arithmetic: 20.5 us -> 27.4 us
    psum x1 -> x0, waiting for transfers between devices: 187 us -> none  [per_device(): lax.psum((grad_w_query, grad_w_key, grad_w_value, grad_w_out, grad_w_in,...]
    pallas_call x0 -> x1, Pallas kernels: none -> 95.5 us  [reduce_all(): pl.pallas_call(functools.partial(reduce_kernel, plan, chunks), out_shape=...]
    psum x1 -> x0, blocking collectives: 41.2 us -> none  [per_device(): lax.psum((grad_w_query, grad_w_key, grad_w_value, grad_w_out, grad_w_in,...]
    slice x0 -> x4, local copies, waits for them, and re-layouts: none -> 7.95 us  [the longest x1 4.2 us: per_device(): sum_back = flat[4 * width + ff:]]
    unnamed x69 -> x67, local copies, waits for them, and re-layouts: 21.2 us -> 13.7 us
    reduce_scatter x1, waiting for transfers between devices: 28.7 us -> 22.7 us  [per_device(): lax.psum_scatter(grad_keys_all.astype(jnp.bfloat16), 'blk', scatter_dimen...]
  transfers between devices with their start and end apart: 5 -> 4, of which waited for: 5 -> 4; matrix products, arithmetic and copies ran while one was open for 6% -> 7% of each run, Pallas kernels for 0% -> 0%
where the time goes in v1:
time: 458 us; the launch traced here: 456 us
  waiting for transfers between devices  151 us (33%)
  matrix products  105 us (23%)
  Pallas kernels  95.5 us (21%)
  local copies, waits for them, and re-layouts  59.3 us (13%)
  other arithmetic  27.4 us (6%)
  between operations  15.5 us (3%)
    pallas_call x1, Pallas kernels, reduce_all(): pl.pallas_call(functools.partial(reduce_kernel, plan, chunks), out_shape=...  95.5 us
    all_gather x1, waiting for transfers between devices, per_device(): value_piece = lax.all_gather(value_bf, 'blk', axis=1, tiled=True)  46.6 us
    reduce_scatter x1, waiting for transfers between devices, per_device(): lax.psum_scatter(grad_values_all.astype(jnp.bfloat16), 'blk', scatter_dim...  43 us
    dot_general x18, matrix products, project(): return jnp.dot(left, right, preferred_element_type=jnp.float32)  42.2 us
    all_gather x1, waiting for transfers between devices, per_device(): key_piece = lax.all_gather(key_bf, 'blk', axis=1, tiled=True)  38.2 us
    reduce_scatter x1, waiting for transfers between devices, per_device(): lax.psum_scatter(grad_keys_all.astype(jnp.bfloat16), 'blk', scatter_dimen...  22.7 us
    unnamed x67, local copies, waits for them, and re-layouts  13.7 us
    dot_general x2, matrix products, back_step(): jnp.einsum('shqk,sqhe->skhe', probs.astype(jnp.bfloat16), grad_attn_heads...  12.3 us
  transfers between devices with their start and end apart: 4, of which 4 were waited for; matrix products, arithmetic and copies ran while one was open for 7% of the time, Pallas kernels for 0%

profile of v1, /device:TPU:0, one launch (start us, length us, event | category | flops | bytes accessed | tf_op | source)
XLA Modules:
  0.0 456.4 jit_solution(1769167977018357368)
XLA Ops:
  19.0 2.0 fusion.47
  21.0 38.2 %all-gather.3.cloned.1.call-done = bf16[2,1024,512]{1,2,0:T(8,128)(2,1)} async-done(((bf16[2,256,512]{1,2,0:T(8,128)(2,1)}), bf16[2,1024,512]{1,2,0:T(8,128)(2,1)}) %all-gather.3.cloned.1.call-update) | async-done | bytes 2097168 | tf_op jit(solution)/shard_map/all_gather | solution.py:272
  59.2 46.6 %all-gather.5.cloned.1.call-done = bf16[2,1024,512]{1,2,0:T(8,128)(2,1)} async-done(((bf16[2,256,512]{1,2,0:T(8,128)(2,1)}), bf16[2,1024,512]{1,2,0:T(8,128)(2,1)}) %all-gather.5.cloned.1.call-update) | async-done | bytes 2097168 | tf_op jit(solution)/shard_map/all_gather | solution.py:273
  105.8 39.1 %while.30 = (s32[]{:T(128)}, f32[2,8,256]{2,1,0:T(8,128)S(1)}, f32[2,8,256]{2,1,0:T(8,128)S(1)}, f32[2,8,256,64]{2,3,1,0:T(8,128)}, s32[2]{0:T(128)S(1)}, /*inde...) while((s32[]{:T(128)}, f32[2,8,256]{2,1,0:T(8,128)S(1)}, ...), condition=%wide.region_3.4_spmd.clone, body=%wide.region_0.3_spmd.clone.sunk | while | flops 565335808 | bytes 69216512 | solution.py:307
  107.5 2.7 constant_dynamic-slice_fusion.7
  110.2 4.8 %fusion.130 = (f32[2,8,256]{2,1,0:T(8,128)S(1)}, f32[2,8,512,256]{3,2,1,0:T(8,128)}) fusion(pred[2,256,512]{1,2,0:T(8,128)(4,1)S(1)} %broadcast_and_fusion.4, bf16[2,512,8,64]{1,3,2,0:T(8,128)(2,1)S(1)} %bitcast.221, bf16[2,256,8,64]{1,3,2,0:T(8,128)(2,1)S(1)} %get-tuple-element.559), kind=kOutput, calls=%fused_computation.4.clone.1 | convolution fusion | flops 274722816 | bytes 10240000 | tf_op jit(solution)/shard_map/while/body/eval_jaxpr/sqhe,skhe->shqk/dot_general | solution.py:288
  115.0 5.1 %fusion.131 = f32[2,8,256]{2,1,0:T(8,128)S(1)} fusion(f32[2,8,512,256]{3,2,1,0:T(8,128)} %get-tuple-element.505, f32[2,8,256]{2,1,0:T(8,128)S(1)} %select_maximum_fusion.2, pred[2,256,512]{1,2,0:T(8,128)(4,1)S(1)} %broadcast_and_fusion.4), kind=kLoop, calls=%fused_computation.6.clone.1 | loop fusion | flops 10481664 | bytes 8683520 | tf_op jit(solution)/shard_map/while/body/eval_jaxpr/reduce_sum | solution.py:297
  120.8 4.4 fusion.133
  126.9 2.7 constant_dynamic-slice_fusion.7
  129.5 4.8 %fusion.130 = (f32[2,8,256]{2,1,0:T(8,128)S(1)}, f32[2,8,512,256]{3,2,1,0:T(8,128)}) fusion(pred[2,256,512]{1,2,0:T(8,128)(4,1)S(1)} %broadcast_and_fusion.4, bf16[2,512,8,64]{1,3,2,0:T(8,128)(2,1)S(1)} %bitcast.221, bf16[2,256,8,64]{1,3,2,0:T(8,128)(2,1)S(1)} %get-tuple-element.559), kind=kOutput, calls=%fused_computation.4.clone.1 | convolution fusion | flops 274722816 | bytes 10240000 | tf_op jit(solution)/shard_map/while/body/eval_jaxpr/sqhe,skhe->shqk/dot_general | solution.py:288
  134.3 5.1 %fusion.131 = f32[2,8,256]{2,1,0:T(8,128)S(1)} fusion(f32[2,8,512,256]{3,2,1,0:T(8,128)} %get-tuple-element.505, f32[2,8,256]{2,1,0:T(8,128)S(1)} %select_maximum_fusion.2, pred[2,256,512]{1,2,0:T(8,128)(4,1)S(1)} %broadcast_and_fusion.4), kind=kLoop, calls=%fused_computation.6.clone.1 | loop fusion | flops 10481664 | bytes 8683520 | tf_op jit(solution)/shard_map/while/body/eval_jaxpr/reduce_sum | solution.py:297
  140.2 4.7 %fusion.133 = f32[2,8,256,64]{2,3,1,0:T(8,128)} fusion(bf16[2,512,8,64]{1,3,2,0:T(8,128)(2,1)} %bitcast.224, f32[2,8,512,256]{3,2,1,0:T(8,128)S(1)} %copy-done.1, f32[2,8,256]{2,1,0:T(8,128)S(1)} %select_maximum_fusion.2, pred[2,256,512]{1,2,0:T(8,128)(4,1)S(1)} %broadcast_and_fusion.4, f32[2,8,256,64]{2,3,1,0:T(8,128)} %get-tuple-element.541, ...), kind=kOutput, calls=%fused_computation.9.clone.1 | convolution fusion | flops 279707648 | bytes 11829249 | tf_op jit(solution)/shard_map/while/body/eval_jaxpr/shqk,skhe->shqe/dot_general | solution.py:298
  144.9 3.4 bitcast_convert_fusion
  148.4 2.7 fusion.50
  153.3 4.0 convert_reduce_fusion
  167.9 65.3 %while.31 = (s32[]{:T(128)}, f32[2,256,8,64]{1,3,2,0:T(8,128)}, bf16[2,1024,512]{2,1,0:T(8,128)(2,1)}, bf16[2,1024,512]{2,1,0:T(8,128)(2,1)}, s32[2]{0:T(128)S(1...) while((s32[]{:T(128)}, f32[2,256,8,64]{1,3,2,0:T(8,128)}, ...), condition=%wide.region_6.7_spmd.clone, body=%wide.region_5.6_spmd.clone.sunk | while | flops 1366165248 | bytes 111208880 | solution.py:395
  170.6 2.5 fusion.144
  173.7 4.5 fusion.145
  178.2 4.0 fusion.146
  182.2 6.2 %fusion.147 = bf16[2,8,512,64]{2,3,1,0:T(8,128)(2,1)} fusion(bf16[2,256,8,64]{1,3,2,0:T(8,128)(2,1)S(1)} %copy-done.23, f32[2,8,512,256]{3,2,1,0:T(8,128)} %copy-done.2, f32[2,8,256]{2,1,0:T(8,128)S(1)} %get-tuple-element.608, pred[2,256,512]{1,2,0:T(8,128)(4,1)S(1)} %broadcast_and_fusion.5), kind=kOutput, calls=%fused_computation.30.clone.1 | convolution fusion | flops 276824064 | bytes 10240000 | tf_op jit(solution)/shard_map/while/body/eval_jaxpr/shqk,sqhe->skhe/dot_general | solution.py:371
  188.3 2.3 copy.102
  190.6 4.5 fusion.148
  195.2 2.3 copy.103
  197.5 3.0 constant_dynamic-update-slice_fusion.3
  203.1 2.5 fusion.144
  206.2 4.5 fusion.145
  210.7 4.3 fusion.146
  215.0 6.2 %fusion.147 = bf16[2,8,512,64]{2,3,1,0:T(8,128)(2,1)} fusion(bf16[2,256,8,64]{1,3,2,0:T(8,128)(2,1)S(1)} %copy-done.23, f32[2,8,512,256]{3,2,1,0:T(8,128)} %copy-done.2, f32[2,8,256]{2,1,0:T(8,128)S(1)} %get-tuple-element.608, pred[2,256,512]{1,2,0:T(8,128)(4,1)S(1)} %broadcast_and_fusion.5), kind=kOutput, calls=%fused_computation.30.clone.1 | convolution fusion | flops 276824064 | bytes 10240000 | tf_op jit(solution)/shard_map/while/body/eval_jaxpr/shqk,sqhe->skhe/dot_general | solution.py:371
  221.2 2.3 copy.102
  223.5 4.5 fusion.148
  228.0 2.3 copy.103
  230.3 3.0 constant_dynamic-update-slice_fusion.3
  236.7 6.8 %fusion.48 = (f32[]{:T(128)}, bf16[512,512]{1,0:T(8,128)(2,1)}, f32[]{:T(128)}) fusion(bf16[2,256,512]{2,1,0:T(8,128)(2,1)} %param.29, f32[]{:T(128)S(6)} %copy.139, f32[512,512]{1,0:T(8,128)} %get-tuple-element.367, f32[512]{0:T(512)S(1)} %bitcast.248, bf16[2,256,512]{2,1,0:T(8,128)(2,1)} %param.17, f32[512,512]{1,0:T(8,128)} %copy-done.7, ...), kind=kOutput, calls=%fused_computation.89 | convolution fusion | flops 1087635456 | bytes 9975820 | tf_op jit(solution)/shard_map/dot_general | solution.py:233
  244.9 2.6 fusion.46
  247.6 2.7 convolution_add_fusion.2
  250.3 2.6 convolution_convert_fusion.1
  252.9 22.7 %reduce-scatter.3.cloned.1.call-done = bf16[2,256,512]{2,1,0:T(8,128)(2,1)} async-done(((bf16[2,1024,512]{2,1,0:T(8,128)(2,1)}), bf16[2,256,512]{2,1,0:T(8,128)(2,1)}) %reduce-scatter.3.cloned.1.call-update) | async-done | bytes 524304 | tf_op jit(solution)/shard_map/reduce_scatter | solution.py:398
  275.6 2.5 fusion.44
  278.1 43.0 %reduce-scatter.5.cloned.1.call-done = bf16[2,256,512]{2,1,0:T(8,128)(2,1)} async-done(((bf16[2,1024,512]{2,1,0:T(8,128)(2,1)}), bf16[2,256,512]{2,1,0:T(8,128)(2,1)}) %reduce-scatter.5.cloned.1.call-update) | async-done | bytes 524304 | tf_op jit(solution)/shard_map/reduce_scatter | solution.py:401
  321.0 2.6 fusion.42
  323.7 2.3 fusion.37
  329.8 1.9 slice_dynamic-update-slice_fusion.1
  333.5 3.6 fusion.36
  337.1 95.5 %grad_sum.1 = (bf16[6,1024,512]{2,1,0:T(8,128)(2,1)}, f32[8,512]{1,0:T(8,128)S(1)}) custom-call(bf16[6,1024,512]{2,1,0:T(8,128)(2,1)} %bitcast.231, f32[8,512]{1,0:T(8,128)S(1)} %concatenate.10.small_in), custom_call_target="tpu_custom_call" | custom-call | tf_op jit(solution)/shard_map/grad_sum/pallas_call | solution.py:204
  432.5 4.5 convert_element_type.181
  437.1 4.2 slice.88
  442.4 2.7 fusion.54
  447.4 2.4 pad_maximum_fusion
  (173 shorter events, 45.6 us)
Async XLA Ops:
  7.2 146.1 %copy-start = (bf16[2048,512]{1,0:T(8,128)(2,1)S(1)}, bf16[2048,512]{1,0:T(8,128)(2,1)}, u32[]{:S(2)}) copy-start(bf16[2048,512]{1,0:T(8,128)(2,1)} %param.25) | copy-start | bytes 6291460
  7.2 7.1 %copy-start.9 = (bf16[2,256,512]{2,1,0:T(8,128)(2,1)S(1)}, bf16[2,256,512]{2,1,0:T(8,128)(2,1)}, u32[]{:S(2)}) copy-start(bf16[2,256,512]{2,1,0:T(8,128)(2,1)} %param.17) | copy-start | bytes 1572868
  7.2 7.0 %copy-start.27 = (s32[2]{0:T(128)S(1)}, s32[2]{0:T(128)}, u32[]{:S(2)}) copy-start(s32[2]{0:T(128)} %param.18) | copy-start | bytes 28
  7.2 52.0 %all-gather.3.cloned.1.call-start = ((), (), s32[]{:S(2)}) async-start(), calls=%async_computation.2 | async-start | bytes 2621440 | tf_op jit(solution)/shard_map/all_gather | solution.py:272
  10.1 95.7 %all-gather.5.cloned.1.call-start = ((), (), s32[]{:S(2)}) async-start(), calls=%async_computation.3 | async-start | bytes 2621440 | tf_op jit(solution)/shard_map/all_gather | solution.py:273
  12.8 262.8 %reduce-scatter.3.cloned.1.call-start = ((), (), s32[]{:S(2)}) async-start(), calls=%async_computation.4 | async-start | bytes 2621440 | tf_op jit(solution)/shard_map/reduce_scatter | solution.py:398
  14.2 91.6 %copy-start.28 = (s32[256]{0:T(256)}, s32[256]{0:T(256)S(1)}, u32[]{:S(2)}) copy-start(s32[256]{0:T(256)S(1)} %iota_add_fusion.4) | copy-start | bytes 3076
  115.0 5.8 %copy-start.1 = (f32[2,8,512,256]{3,2,1,0:T(8,128)S(1)}, f32[2,8,512,256]{3,2,1,0:T(8,128)}, u32[]{:S(2)}) copy-start(f32[2,8,512,256]{3,2,1,0:T(8,128)} %get-tuple-element.505) | copy-start | bytes 25165828 | tf_op jit(solution)/shard_map/while
  134.3 5.8 %copy-start.1 = (f32[2,8,512,256]{3,2,1,0:T(8,128)S(1)}, f32[2,8,512,256]{3,2,1,0:T(8,128)}, u32[]{:S(2)}) copy-start(f32[2,8,512,256]{3,2,1,0:T(8,128)} %get-tuple-element.505) | copy-start | bytes 25165828 | tf_op jit(solution)/shard_map/while
  144.9 7.0 %copy-start.15 = (bf16[512,2048]{1,0:T(8,128)(2,1)S(1)}, bf16[512,2048]{1,0:T(8,128)(2,1)}, u32[]{:S(2)}) copy-start(bf16[512,2048]{1,0:T(8,128)(2,1)} %param.23) | copy-start | bytes 6291460
  148.4 2.7 copy-start.10
  151.1 0.8 copy-start.19
  151.1 2.1 copy-start.24
  151.1 2.1 copy-start.30
  153.3 4.0 copy-start.12
  153.3 4.0 copy-start.17
  157.3 1.4 copy-start.32
  157.3 2.3 copy-start.16
  158.7 1.0 copy-start.7
  167.9 1.3 copy-start.3
  170.6 3.0 copy-start.5
  170.6 3.1 copy-start.22
  173.1 5.1 %copy-start.2 = (f32[2,8,512,256]{3,2,1,0:T(8,128)}, f32[2,8,512,256]{3,2,1,0:T(8,128)S(1)}, u32[]{:S(2)}) copy-start(f32[2,8,512,256]{3,2,1,0:T(8,128)S(1)} %fusion.144) | copy-start | bytes 25165828 | tf_op jit(solution)/shard_map/while
  178.2 4.0 copy-start.23
  182.2 8.5 %copy-start.4 = (bf16[2,256,8,64]{1,3,2,0:T(8,128)(2,1)S(1)}, bf16[2,256,8,64]{1,3,2,0:T(8,128)(2,1)}, u32[]{:S(2)}) copy-start(bf16[2,256,8,64]{1,3,2,0:T(8,128)(2,1)} %copy-done.3) | copy-start | bytes 1572868 | tf_op jit(solution)/shard_map/while
  200.4 1.3 copy-start.3
  203.1 3.0 copy-start.5
  203.1 3.1 copy-start.22
  205.6 5.1 %copy-start.2 = (f32[2,8,512,256]{3,2,1,0:T(8,128)}, f32[2,8,512,256]{3,2,1,0:T(8,128)S(1)}, u32[]{:S(2)}) copy-start(f32[2,8,512,256]{3,2,1,0:T(8,128)S(1)} %fusion.144) | copy-start | bytes 25165828 | tf_op jit(solution)/shard_map/while
  210.7 4.3 copy-start.23
  215.0 8.5 %copy-start.4 = (bf16[2,256,8,64]{1,3,2,0:T(8,128)(2,1)S(1)}, bf16[2,256,8,64]{1,3,2,0:T(8,128)(2,1)}, u32[]{:S(2)}) copy-start(bf16[2,256,8,64]{1,3,2,0:T(8,128)(2,1)} %copy-done.3) | copy-start | bytes 1572868 | tf_op jit(solution)/shard_map/while
  233.2 0.7 copy-start.29
  233.3 1.9 copy-start.6
  233.3 3.5 copy-start.31
  233.3 87.7 %reduce-scatter.5.cloned.1.call-start = ((), (), s32[]{:S(2)}) async-start(), calls=%async_computation.5 | async-start | bytes 2621440 | tf_op jit(solution)/shard_map/reduce_scatter | solution.py:401
  236.7 10.9 %copy-start.8 = (f32[512,512]{1,0:T(8,128)S(1)}, f32[512,512]{1,0:T(8,128)}, u32[]{:S(2)}) copy-start(f32[512,512]{1,0:T(8,128)} %copy-done.7) | copy-start | bytes 3145732
  244.9 5.4 %copy-start.20 = (bf16[512,512]{1,0:T(8,128)(2,1)S(1)}, bf16[512,512]{1,0:T(8,128)(2,1)}, u32[]{:S(2)}) copy-start(bf16[512,512]{1,0:T(8,128)(2,1)} %copy-done.19) | copy-start | bytes 1572868
  244.9 5.3 %copy-start.33 = (bf16[512,2048]{1,0:T(8,128)(2,1)S(1)}, bf16[512,2048]{1,0:T(8,128)(2,1)}, u32[]{:S(2)}) copy-start(bf16[512,2048]{1,0:T(8,128)(2,1)} %copy-done.32) | copy-start | bytes 6291460
  321.0 12.5 %copy-start.13 = (f32[512,2048]{1,0:T(8,128)S(1)}, f32[512,2048]{1,0:T(8,128)}, u32[]{:S(2)}) copy-start(f32[512,2048]{1,0:T(8,128)} %copy-done.12) | copy-start | bytes 12582916
  321.0 12.5 %copy-start.25 = (bf16[512,512]{1,0:T(8,128)(2,1)S(1)}, bf16[512,512]{1,0:T(8,128)(2,1)}, u32[]{:S(2)}) copy-start(bf16[512,512]{1,0:T(8,128)(2,1)} %fusion.47) | copy-start | bytes 1572868
  442.4 3.3 copy-start.11
  442.4 3.3 copy-start.18
  442.4 3.3 copy-start.26
  442.4 3.8 copy-start.14
  442.4 3.8 copy-start.21
Sparse Core Ops, SparseCore 0:
  10.2 48.9 all-gather.2
  61.3 44.4 all-gather.4
  233.4 42.1 reduce-scatter.2
  277.8 43.1 reduce-scatter.4

commit v2 on v1

v2 whole, which is shorter than its diff:
```python
import functools

import jax
import jax.numpy as jnp
from jax import lax
from jax.experimental import pallas as pl
from jax.experimental.pallas import tpu as pltpu
from jax.sharding import PartitionSpec as P

HEADS = 8
HEAD_DIM = 64
PAIR = 2 * HEAD_DIM

MESH = pl.DeviceIdType.MESH


class Reducer:
    def __init__(self, nb, nz, rows):
        self.rows = rows
        plane = [("batch", 1 << i) for i in range(1, nb.bit_length() - 1)]
        line = [("blk", 1 << i) for i in range(nz.bit_length() - 1)]
        self.orders = [plane + line, plane[::-1] + line]
        self.all_bits = [("batch", 1)] + plane + line
        self.steps = len(self.orders[0])
        self.halves = 0
        length, land = rows // 4, rows // 2
        self.sizes, self.lands = [], [[], []]
        for _ in range(self.steps):
            if length >= 32:
                length //= 2
                self.halves += 1
            self.sizes.append(length)
            for o in (0, 1):
                self.lands[o].append(land)
                land += length
        self.land_rows = land
        self.sems = 2 + 4 * self.steps

    def scratch(self, chunks, width):
        return [
            pltpu.VMEM((chunks, self.land_rows, width), jnp.bfloat16),
            pltpu.SemaphoreType.DMA((chunks, self.sems)),
            pltpu.SemaphoreType.DMA((chunks, self.sems)),
        ]

    def bind(self, grads, total, land, send_sem, recv_sem):
        self.grads, self.total, self.land = grads, total, land
        self.send_sem, self.recv_sem = send_sem, recv_sem
        self.at = {"batch": lax.axis_index("batch"), "blk": lax.axis_index("blk")}
        core = self.at["batch"] % 2
        half = self.rows // 2
        self.core_keep, self.core_send = core * half, (1 - core) * half
        self.keep, self.send, self.own = [[], []], [[], []], []
        for o in (0, 1):
            off = self.core_keep + o * (half // 2)
            for i, (axis, bit) in enumerate(self.orders[o]):
                mine = (self.at[axis] // bit) % 2
                if i < self.halves:
                    self.keep[o].append(off + mine * self.sizes[i])
                    self.send[o].append(off + (1 - mine) * self.sizes[i])
                    off = self.keep[o][-1]
                else:
                    self.keep[o].append(off)
                    self.send[o].append(off)
            self.own.append(off)

    def partner(self, axis, bit):
        mine = (self.at[axis] // bit) % 2
        there = self.at[axis] + bit * (1 - 2 * mine)
        if axis == "batch":
            return (there, self.at["blk"])
        return (self.at["batch"], there)

    def copy(self, c, src, src_row, dst, dst_row, size, sem, axis, bit):
        return pltpu.make_async_remote_copy(
            src_ref=src.at[c, pl.ds(pl.multiple_of(src_row, 16), size)],
            dst_ref=dst.at[c, pl.ds(pl.multiple_of(dst_row, 16), size)],
            send_sem=self.send_sem.at[c, sem],
            recv_sem=self.recv_sem.at[c, sem],
            device_id=self.partner(axis, bit),
            device_id_type=MESH,
        )

    def core_out(self, c):
        return self.copy(c, self.grads, self.core_send, self.land, 0, self.rows // 2, 0, "batch", 1)

    def core_back(self, c):
        return self.copy(
            c, self.total, self.core_keep, self.total, self.core_keep, self.rows // 2, 1, "batch", 1
        )

    def out(self, c, o, i):
        axis, bit = self.orders[o][i]
        return self.copy(
            c, self.grads, self.send[o][i], self.land, self.lands[o][i], self.sizes[i],
            2 + o * self.steps + i, axis, bit,
        )

    def back(self, c, o, i):
        axis, bit = self.orders[o][i]
        row = self.keep[o][i]
        return self.copy(
            c, self.total, row, self.total, row, self.sizes[i],
            2 + (2 + o) * self.steps + i, axis, bit,
        )

    def add(self, c, row, land_row, size, last=False):
        piece = min(size, 64)
        target = self.total if last else self.grads

        def body(k, carry):
            here = pl.ds(pl.multiple_of(row + k * piece, 16), piece)
            there = pl.ds(pl.multiple_of(land_row + k * piece, 16), piece)
            target[c, here] = self.grads[c, here] + self.land[c, there]
            return carry

        lax.fori_loop(0, size // piece, body, 0)

    def stages(self):
        return 2 * self.steps + 3 - (self.steps - self.halves)

    def stage(self, k, c):
        n = self.steps
        if k == 0:
            self.core_out(c).start()
        elif k <= n + 1:
            i = k - 2
            if k == 1:
                self.core_out(c).wait()
                self.add(c, self.core_keep, 0, self.rows // 2)
            else:
                for o in (0, 1):
                    self.out(c, o, i).wait()
                    self.add(c, self.keep[o][i], self.lands[o][i], self.sizes[i], i == n - 1)
            if i + 1 < n:
                for o in (0, 1):
                    self.out(c, o, i + 1).start()
            else:
                for o in (0, 1):
                    self.back(c, o, self.halves - 1).start()
        elif k < self.stages() - 1:
            i = self.halves - 1 - (k - n - 2)
            for o in (0, 1):
                self.back(c, o, i).wait()
            if i > 0:
                for o in (0, 1):
                    self.back(c, o, i - 1).start()
            else:
                self.core_back(c).start()
        else:
            self.core_back(c).wait()

    def small_copy(self, small, land, send_sem, recv_sem, i):
        axis, bit = self.all_bits[i]
        return pltpu.make_async_remote_copy(
            src_ref=small.at[i],
            dst_ref=land.at[i],
            send_sem=send_sem.at[i],
            recv_sem=recv_sem.at[i],
            device_id=self.partner(axis, bit),
            device_id_type=MESH,
        )


BF = jnp.bfloat16
F32 = jnp.float32
NEG = -1e30


def mm(left, right):
    return jnp.dot(left, right, preferred_element_type=F32)


def mm_nt(left, right):
    return lax.dot_general(left, right, (((1,), (1,)), ((), ())), preferred_element_type=F32)


def layer_kernel(plan, n, keep, lens, alphas, *refs):
    (
        tokens, cot, wq, wk, wv, wo, w_in, b_in, w_back, b_back,
        outputs, grad_input, total, small_out,
        x_all, wk_t, wv_t, x_t, k_all, v_all, k_t, v_t, q_m, do_m, top, norm, o_t, attn_t, do_t,
        live_branch, resid, resid_bf, resid_t, grad_ffn, ffn, grad_x, lse, delta,
        dq_t, dk, dv, acc, back_in,
        x_send, x_recv, r_send, r_recv,
        grads, land, send_sem, recv_sem, small, small_land, small_send, small_recv,
    ) = refs
    seqs, rows, width = tokens.shape
    chunks = grads.shape[0]
    ff_chunks = w_in.shape[1] // width
    pairs = width // PAIR
    plan.bind(grads, total, land, send_sem, recv_sem)
    b, z = lax.axis_index("batch"), lax.axis_index("blk")
    has_up, has_down = z < n - 1, z > 0
    alpha_attn, alpha_ffn = alphas[0], alphas[1]

    def x_copy(s, j):
        return pltpu.make_async_remote_copy(
            src_ref=x_all.at[s, j], dst_ref=x_all.at[s, j],
            send_sem=x_send.at[s, j], recv_sem=x_recv.at[s, j],
            device_id=(b, z + 1), device_id_type=MESH,
        )

    def r_copy(s, j, src):
        return pltpu.make_async_remote_copy(
            src_ref=src.at[s, j], dst_ref=back_in.at[s, j],
            send_sem=r_send.at[s, j], recv_sem=r_recv.at[s, j],
            device_id=(b, z - 1), device_id_type=MESH,
        )

    barrier = pltpu.get_barrier_semaphore()
    for axis, bit in plan.all_bits:
        pl.semaphore_signal(barrier, inc=1, device_id=plan.partner(axis, bit), device_id_type=MESH)

    @pl.when(has_up)
    def _():
        pl.semaphore_signal(barrier, inc=1, device_id=(b, z + 1), device_id_type=MESH)

    @pl.when(has_down)
    def _():
        pl.semaphore_signal(barrier, inc=1, device_id=(b, z - 1), device_id_type=MESH)

    for s in range(seqs):
        x_all[s, z] = tokens[s]
    pl.semaphore_wait(barrier, len(plan.all_bits) + jnp.where(has_up, 1, 0) + jnp.where(has_down, 1, 0))

    @pl.when(has_up)
    def _():
        for s in range(seqs):
            x_copy(s, z).start()

    wk_t[...] = wk[...].T
    wv_t[...] = wv[...].T
    small[0] = jnp.zeros_like(small[0])
    acc[...] = jnp.zeros_like(acc)
    low_lanes = lax.broadcasted_iota(jnp.int32, (rows, PAIR), 1) < HEAD_DIM
    key_iota = lax.broadcasted_iota(jnp.int32, (rows, rows), 0)
    query_pos = z * rows + lax.broadcasted_iota(jnp.int32, (1, rows), 1)

    def split_heads(value, target, s):
        for h in range(HEADS):
            pair = value[:, (h // 2) * PAIR : (h // 2 + 1) * PAIR]
            mask = low_lanes if h % 2 == 0 else jnp.logical_not(low_lanes)
            target[s, h] = jnp.where(mask, pair, 0.0).astype(BF)

    def slot(s, j):
        return s * n + j if keep else 0

    def project(s, j):
        here = slot(s, j)
        x = x_all[s, j]
        k_all[here] = mm(x, wk[...]).astype(BF)
        v_all[here] = mm(x, wv[...]).astype(BF)
        k_t[here] = mm_nt(wk_t[...], x).astype(BF)
        v_t[here] = mm_nt(wv_t[...], x).astype(BF)
        x_t[here] = x.T

    def allowed(s, j):
        limit = jnp.minimum(query_pos + 1, lens[s]) - j * rows
        return key_iota < limit

    def head_rows(head):
        return pl.ds(pl.multiple_of(head * HEAD_DIM, HEAD_DIM), HEAD_DIM)

    def pair_lanes(p):
        return pl.ds(pl.multiple_of(p * PAIR, PAIR), PAIR)

    def forward_tile(s, j):
        here = slot(s, j)
        mask = allowed(s, j)

        def pair_step(p, carry):
            keys = k_all[here, :, pair_lanes(p)]
            for h in (0, 1):
                head = 2 * p + h
                scores = jnp.where(mask, mm_nt(keys, q_m[s, head]), NEG)
                old = top[s, head]
                new = jnp.maximum(old, jnp.max(scores, axis=0, keepdims=True))
                weights = jnp.exp(scores - new)
                factor = jnp.exp(old - new)
                top[s, head] = new
                norm[s, head] = norm[s, head] * factor + jnp.sum(weights, axis=0, keepdims=True)
                part = mm(v_t[here, head_rows(head)], weights.astype(BF))
                o_t[s, head_rows(head)] = o_t[s, head_rows(head)] * factor + part
            return carry

        lax.fori_loop(0, pairs, pair_step, 0)

    def pass_on(s, j):
        x_copy(s, j).wait_recv()

        @pl.when(has_up)
        def _():
            x_copy(s, j).start()

    early = 2

    def start_seq(s):
        q = mm(x_all[s, z], wq[...]).astype(BF).astype(F32) * 0.125
        split_heads(q, q_m, s)
        top[s] = jnp.full_like(top[s], NEG)
        norm[s] = jnp.zeros_like(norm[s])
        o_t[s] = jnp.zeros_like(o_t[s])
        project(s, z)
        forward_tile(s, z)

    def attention(s):
        def block(i, carry):
            if s == 0:
                pass_on(s, z - i)
            else:
                @pl.when((i > early) | jnp.logical_not(has_up))
                def _():
                    pass_on(s, z - i)
            project(s, z - i)
            forward_tile(s, z - i)
            return carry

        lax.fori_loop(1, z + 1, block, 0)
        for h in range(HEADS):
            here = slice(h * HEAD_DIM, (h + 1) * HEAD_DIM)
            o_t[s, here] = o_t[s, here] / norm[s, h]
            lse[s, h] = top[s, h] + jnp.log(norm[s, h])
        attn_t[s] = o_t[s].astype(BF)
        branch = mm(attn_t[s].T, wo[...])
        position = z * rows + lax.broadcasted_iota(jnp.int32, (rows, 1), 0)
        live = (position < lens[s]).astype(F32)
        live_branch[s] = live * branch
        resid[...] = tokens[s].astype(F32) + alpha_attn * live_branch[s]
        resid_bf[...] = resid[...].astype(BF)
        resid_t[...] = resid_bf[...].T

    def feed_forward(s):
        grad_out = cot[s].astype(F32)
        grad_ffn[...] = (alpha_ffn * grad_out).astype(BF)
        ffn[...] = jnp.zeros_like(ffn)
        grad_x[s] = grad_out
        small[0, ff_chunks : ff_chunks + 1] += jnp.sum(
            grad_ffn[...].astype(F32), axis=0, keepdims=True
        )

        def column(c, carry):
            if s == 0:
                for i in range(1, early + 1):
                    @pl.when((c == 2 * (i - 1)) & (z >= i) & has_up)
                    def _():
                        pass_on(1, z - i)
            lanes = pl.ds(pl.multiple_of(c * width, width), width)
            hidden = mm(resid_bf[...], w_in[:, lanes]) + b_in[pl.ds(c, 1)]
            square = hidden * hidden
            tan = jnp.tanh(0.7978845608 * hidden * (1.0 + 0.044715 * square))
            half = 0.5 * (1.0 + tan)
            act = (hidden * half).astype(BF)
            slope = half + 0.5 * hidden * (1.0 - tan * tan) * (
                0.7978845608 * (1.0 + 3 * 0.044715 * square)
            )
            back = w_back[lanes]
            ffn[...] += mm(act, back)
            grad_hidden = (mm_nt(grad_ffn[...], back) * slope).astype(BF)
            small[0, pl.ds(c, 1)] += jnp.sum(grad_hidden.astype(F32), axis=0, keepdims=True)
            grad_x[s] += mm_nt(grad_hidden, w_in[:, lanes])
            grad_back = mm(act.T, grad_ffn[...])
            grad_in = mm(resid_t[...], grad_hidden)
            if s > 0:
                grad_back += grads[c, :width].astype(F32)
                grad_in += grads[c, width:].astype(F32)
            grads[c, :width] = grad_back.astype(BF)
            grads[c, width:] = grad_in.astype(BF)
            return carry

        lax.fori_loop(0, ff_chunks, column, 0)
        ffn_out = ffn[...] + b_back[...]
        outputs[s] = (resid[...] + alpha_ffn * ffn_out).astype(BF)
        small[0, ff_chunks + 2 : ff_chunks + 3] += jnp.sum(
            cot[s].astype(F32) * ffn_out, axis=0, keepdims=True
        )
        small[0, ff_chunks + 1 : ff_chunks + 2] += jnp.sum(
            grad_x[s] * live_branch[s], axis=0, keepdims=True
        )

    def attention_back(s):
        position = z * rows + lax.broadcasted_iota(jnp.int32, (rows, 1), 0)
        live = (position < lens[s]).astype(F32)
        grad_branch = (alpha_attn * live * grad_x[s]).astype(BF)
        acc[0] += mm(attn_t[s], grad_branch)
        do = mm_nt(grad_branch, wo[...]).astype(BF)
        split_heads(do, do_m, 0)
        do_t[...] = mm_nt(wo[...], grad_branch).astype(BF)
        for h in range(HEADS):
            here = slice(h * HEAD_DIM, (h + 1) * HEAD_DIM)
            delta[h] = jnp.sum(do_t[here].astype(F32) * o_t[s, here], axis=0, keepdims=True)
        dq_t[...] = jnp.zeros_like(dq_t)

        def block(j, carry):
            here = slot(s, j)
            if not keep:
                project(s, j)
            mask = allowed(s, j)

            def pair_step(p, carry_pair):
                keys = k_all[here, :, pair_lanes(p)]
                values = v_all[here, :, pair_lanes(p)]
                grad_key = jnp.zeros((rows, PAIR), F32)
                grad_value = jnp.zeros((rows, PAIR), F32)
                for h in (0, 1):
                    head = 2 * p + h
                    scores = mm_nt(keys, q_m[s, head])
                    probs = jnp.where(mask, jnp.exp(scores - lse[s, head]), 0.0)
                    grad_probs = mm_nt(values, do_m[0, head])
                    grad_scores = (probs * (grad_probs - delta[head])).astype(BF)
                    grad_value += mm(probs.astype(BF), do_m[0, head])
                    grad_key += mm(grad_scores, q_m[s, head])
                    dq_t[head_rows(head)] += mm(k_t[here, head_rows(head)], grad_scores)
                dk[:, pair_lanes(p)] = grad_key.astype(BF)
                dv[:, pair_lanes(p)] = grad_value.astype(BF)
                return carry_pair

            lax.fori_loop(0, pairs, pair_step, 0)
            part = mm_nt(dk[...], wk[...]) + mm_nt(dv[...], wv[...])
            acc[2] += mm(x_t[here], dk[...])
            acc[3] += mm(x_t[here], dv[...])

            @pl.when(j < z)
            def _():
                x_all[s, j] = part.astype(BF)

                @pl.when(jnp.logical_not(has_up))
                def _():
                    r_copy(s, j, x_all).start()

            @pl.when(j == z)
            def _():
                grad_x[s] += part

            return carry

        @pl.when(has_up)
        def _():
            def sent(j, carry):
                x_copy(s, j).wait_send()
                return carry

            lax.fori_loop(0, z + 1, sent, 0)

        lax.fori_loop(0, z + 1, block, 0)
        dq = (dq_t[...] * 0.125).T.astype(BF)
        if not keep:
            x_t[0] = tokens[s].T
        acc[1] += mm(x_t[slot(s, z)], dq)
        grad_x[s] += mm_nt(dq, wq[...])

    def send_back(s):
        def block(j, carry):
            @pl.when(has_up)
            def _():
                r_copy(s, j, back_in).wait_recv()

                @pl.when(j < z)
                def _():
                    back_in[s, j] = back_in[s, j] + x_all[s, j]
                    r_copy(s, j, back_in).start()

            return carry

        lax.fori_loop(0, z + 1, block, 0)

        @pl.when(has_up)
        def _():
            grad_input[s] = (grad_x[s] + back_in[s, z].astype(F32)).astype(BF)

        @pl.when(jnp.logical_not(has_up))
        def _():
            grad_input[s] = grad_x[s].astype(BF)

    for s in range(seqs):
        start_seq(s)
    for s in range(seqs):
        attention(s)
        feed_forward(s)
    for s in range(seqs):
        attention_back(s)
    for k in range(4):
        place = 2 * ff_chunks + k
        grads[place // 2, pl.ds((place % 2) * width, width)] = acc[k].astype(BF)
    for s in range(seqs):
        send_back(s)

    def tick(t, carry):
        for k in range(plan.stages() - 1, -1, -1):
            c = t - k

            @pl.when((c >= 0) & (c < chunks))
            def _():
                plan.stage(k, c)

        return carry

    lax.fori_loop(0, chunks + plan.stages() - 1, tick, 0)
    steps = len(plan.all_bits)
    for i in range(steps):
        plan.small_copy(small, small_land, small_send, small_recv, i).start()
        plan.small_copy(small, small_land, small_send, small_recv, i).wait()
        small[i + 1] = small[i] + small_land[i]
    small_out[...] = small[steps]

    @pl.when(has_down)
    def _():
        def sent(j, carry):
            for s in range(seqs):
                r_copy(s, j, back_in).wait_send()
            return carry

        lax.fori_loop(0, z, sent, 0)


def per_device(
    tokens, lengths, w_query, w_key, w_value, w_out, w_in, b_in, w_back, b_back,
    alpha_attn, alpha_ffn, cotangent,
):
    seqs, rows, width = tokens.shape
    ff = w_in.shape[1]
    nb, n = lax.axis_size("batch"), lax.axis_size("blk")
    keep = n <= 4
    slots = seqs * n if keep else 1
    ff_chunks = ff // width
    chunks = ff_chunks + 2
    plan = Reducer(nb, n, 2 * width)
    steps = len(plan.all_bits)
    small_rows = -(-(ff_chunks + 3) // 8) * 8
    vmem = pl.BlockSpec(memory_space=pltpu.VMEM)
    smem = pl.BlockSpec(memory_space=pltpu.SMEM)
    square = (rows, width)
    dma = pltpu.SemaphoreType.DMA
    outputs, grad_input, total, small = pl.pallas_call(
        functools.partial(layer_kernel, plan, n, keep),
        out_shape=(
            jax.ShapeDtypeStruct(tokens.shape, BF),
            jax.ShapeDtypeStruct(tokens.shape, BF),
            jax.ShapeDtypeStruct((chunks, 2 * width, width), BF),
            jax.ShapeDtypeStruct((small_rows, width), F32),
        ),
        in_specs=[smem, smem] + [vmem] * 10,
        out_specs=(vmem,) * 4,
        scratch_shapes=[
            pltpu.VMEM((seqs, n) + square, BF),
            pltpu.VMEM((width, width), BF),
            pltpu.VMEM((width, width), BF),
            pltpu.VMEM((slots, width, rows), BF),
            pltpu.VMEM((slots,) + square, BF),
            pltpu.VMEM((slots,) + square, BF),
            pltpu.VMEM((slots, width, rows), BF),
            pltpu.VMEM((slots, width, rows), BF),
            pltpu.VMEM((seqs, HEADS, rows, PAIR), BF),
            pltpu.VMEM((1, HEADS, rows, PAIR), BF),
            pltpu.VMEM((seqs, HEADS, 1, rows), F32),
            pltpu.VMEM((seqs, HEADS, 1, rows), F32),
            pltpu.VMEM((seqs, width, rows), F32),
            pltpu.VMEM((seqs, width, rows), BF),
            pltpu.VMEM((width, rows), BF),
            pltpu.VMEM((seqs,) + square, F32),
            pltpu.VMEM(square, F32),
            pltpu.VMEM(square, BF),
            pltpu.VMEM((width, rows), BF),
            pltpu.VMEM(square, BF),
            pltpu.VMEM(square, F32),
            pltpu.VMEM((seqs,) + square, F32),
            pltpu.VMEM((seqs, HEADS, 1, rows), F32),
            pltpu.VMEM((HEADS, 1, rows), F32),
            pltpu.VMEM((width, rows), F32),
            pltpu.VMEM(square, BF),
            pltpu.VMEM(square, BF),
            pltpu.VMEM((4, width, width), F32),
            pltpu.VMEM((seqs, n) + square, BF),
            dma((seqs, n)), dma((seqs, n)), dma((seqs, n)), dma((seqs, n)),
            pltpu.VMEM((chunks, 2 * width, width), BF),
        ]
        + plan.scratch(chunks, width)
        + [
            pltpu.VMEM((steps + 1, small_rows, width), F32),
            pltpu.VMEM((steps, small_rows, width), F32),
            dma((steps,)),
            dma((steps,)),
        ],
        name="layer",
        compiler_params=pltpu.CompilerParams(
            collective_id=0, has_side_effects=True, vmem_limit_bytes=60 << 20
        ),
    )(
        lengths, jnp.stack([alpha_attn, alpha_ffn]), tokens, cotangent,
        w_query, w_key, w_value, w_out, w_in, b_in.reshape(ff_chunks, width), w_back,
        b_back.reshape(1, width),
    )
    sum_back = total[:ff_chunks, :width].reshape(ff, width).astype(F32)
    sum_in = jnp.concatenate([total[c, width:] for c in range(ff_chunks)], axis=1).astype(F32)
    sum_out, sum_query = total[ff_chunks, :width].astype(F32), total[ff_chunks, width:].astype(F32)
    sum_key, sum_value = total[ff_chunks + 1, :width].astype(F32), total[ff_chunks + 1, width:].astype(F32)
    return (
        outputs, grad_input, sum_query, sum_key, sum_value, sum_out, sum_in,
        small[:ff_chunks].reshape(ff), sum_back, small[ff_chunks],
        jnp.sum(small[ff_chunks + 1]), jnp.sum(small[ff_chunks + 2]),
    )


def solution(mesh):
    return jax.shard_map(
        per_device,
        mesh=mesh,
        in_specs=(
            P("batch", "blk", None),
            P("batch"),
            P(),
            P(),
            P(),
            P(),
            P(),
            P(),
            P(),
            P(),
            P(),
            P(),
            P("batch", "blk", None),
        ),
        out_specs=(
            P("batch", "blk", None),
            P("batch", "blk", None),
            P(),
            P(),
            P(),
            P(),
            P(),
            P(),
            P(),
            P(),
            P(),
            P(),
        ),
        check_vma=False,
    )
```

time: 458 us -> 211 us (0.46)
  waiting for transfers between devices: 151 us -> 0 us
  matrix products: 105 us -> 0 us
  Pallas kernels: 95.5 us -> 191 us
  local copies, waits for them, and re-layouts: 59.3 us -> 5.94 us
  other arithmetic: 27.4 us -> 12.4 us
  between operations: 15.5 us -> 1.95 us
    dot_general x32 -> x0, matrix products: 105 us -> none  [the longest x18 42.2 us: project(): return jnp.dot(left, right, preferred_element_type=jnp.float32)]
    pallas_call x1, Pallas kernels: 95.5 us -> 191 us  [per_device(): pl.pallas_call(functools.partial(layer_kernel, plan, n, keep), out_shape=...]
    all_gather x2 -> x0, waiting for transfers between devices: 84.8 us -> none  [the longest x1 46.6 us: per_device(): value_piece = lax.all_gather(value_bf, 'blk', axis=1, tiled=True)]
    reduce_scatter x2 -> x0, waiting for transfers between devices: 65.6 us -> none  [the longest x1 43 us: per_device(): lax.psum_scatter(grad_values_all.astype(jnp.bfloat16), 'blk', scatter_dim...]
    dynamic_update_slice x6 -> x0, local copies, waits for them, and re-layouts: 15.1 us -> none  [the longest x4 10.6 us: back_step(): lax.dynamic_update_slice_in_dim(grad_values, grad_values_block.reshape(se...]
    reduce_sum x4 -> x1, other arithmetic: 13.1 us -> 2.02 us  [per_device(): jnp.sum(small[ff_chunks + 2])]
    unnamed x67 -> x8, local copies, waits for them, and re-layouts: 13.7 us -> 2.92 us
    dynamic_slice x10 -> x0, local copies, waits for them, and re-layouts: 10.6 us -> none  [the longest x2 5.3 us: one_step(): lax.dynamic_slice_in_dim(value_piece, begin, fold_step_len, 1)]
  transfers between devices with their start and end apart: 4 -> 0, of which waited for: 4 -> 0; matrix products, arithmetic and copies ran while one was open for 7% -> 0% of each run, Pallas kernels for 0% -> 0%
where the time goes in v2:
time: 211 us
  Pallas kernels  191 us (91%)
  other arithmetic  12.4 us (6%)
  local copies, waits for them, and re-layouts  5.94 us (3%)
    pallas_call x1, Pallas kernels, per_device(): pl.pallas_call(functools.partial(layer_kernel, plan, n, keep), out_shape=...  191 us
    squeeze x1, other arithmetic, per_device(): total[c, width:]  4.51 us

profile of v2, /device:TPU:0, one launch (start us, length us, event | category | flops | bytes accessed | tf_op | source)
XLA Modules:
  0.0 210.9 jit_solution(1887361307206405955)
XLA Ops:
  1.9 0.6 pad_maximum_fusion.alphas
  2.5 1.3 reshape.44.refs_7_
  3.8 190.6 %layer.1 = (bf16[2,256,512]{2,1,0:T(8,128)(2,1)}, bf16[2,256,512]{2,1,0:T(8,128)(2,1)}, bf16[6,1024,512]{2,1,0:T(8,128)(2,1)}, f32[8,512]{1,0:T(8,128)}) custom-call(s32[2]{0:T(128)} %lens.1, f32[2]{0:T(128)} %pad_maximum_fusion.alphas, bf16[2,256,512]{2,1,0:T(8,128)(2,1)} %refs_0_.1, bf16[2,256,512]{2,1,0:T(8,128)(2,1)} %refs_1_.1, ...), custom_call_target="tpu_custom_call" | custom-call | tf_op jit(solution)/shard_map/layer/pallas_call | solution.py:534
  194.5 2.0 slice_reduce_fusion
  196.5 0.7 slice_bitcast_fusion.4
  197.2 0.6 copy.25
  197.8 1.7 slice.48
  199.5 4.5 %slice_bitcast_fusion.3 = (bf16[512,512]{1,0:T(8,128)(2,1)S(1)}, bf16[512,512]{1,0:T(8,128)(2,1)S(1)}, bf16[512,512]{1,0:T(8,128)(2,1)S(1)}, bf16[512,512]{1,0:T...) fusion(bf16[6,1024,512]{2,1,0:T(8,128)(2,1)} %get-tuple-element.18), kind=kLoop, calls=%fused_computation.9 | loop fusion | flops 1048576 | bytes 10485760 | tf_op jit(solution)/shard_map/squeeze | solution.py:594
  204.0 2.6 %maximum_convert_fusion = f32[512,2048]{1,0:T(8,128)} fusion(bf16[512,512]{1,0:T(8,128)(2,1)S(1)} %get-tuple-element.23, bf16[512,512]{1,0:T(8,128)(2,1)S(1)} %get-tuple-element.24, bf16[512,512]{1,0:T(8,128)(2,1)S(1)} %get-tuple-element.25, bf16[512,512]{1,0:T(8,128)(2,1)S(1)} %get-tuple-element.22), kind=kLoop, calls=%fused_computation | loop fusion | flops 8388608 | bytes 6291456 | tf_op jit(solution)/shard_map/convert_element_type | solution.py:594
  206.6 0.0 copy-start.1
  206.6 0.0 copy-start
  206.6 2.7 %bitcast_convert_fusion = f32[2048,512]{1,0:T(8,128)} fusion(bf16[4,512,512]{2,1,0:T(8,128)(2,1)S(1)} %slice.48), kind=kLoop, calls=%fused_computation.1 | loop fusion | flops 1048576 | bytes 6291456 | tf_op jit(solution)/shard_map/convert_element_type | solution.py:593
  209.3 0.0 copy-done.1
  209.3 0.8 copy.30
  210.1 0.0 copy-done
  210.1 0.8 copy.31
Async XLA Ops:
  206.6 2.8 %copy-start.1 = (bf16[2,256,512]{2,1,0:T(8,128)(2,1)S(1)}, bf16[2,256,512]{2,1,0:T(8,128)(2,1)}, u32[]{:S(2)}) copy-start(bf16[2,256,512]{2,1,0:T(8,128)(2,1)} %get-tuple-element.43) | copy-start | bytes 1572868
  206.6 3.5 %copy-start = (bf16[2,256,512]{2,1,0:T(8,128)(2,1)S(1)}, bf16[2,256,512]{2,1,0:T(8,128)(2,1)}, u32[]{:S(2)}) copy-start(bf16[2,256,512]{2,1,0:T(8,128)(2,1)} %get-tuple-element.44) | copy-start | bytes 1572868
